TPU v7x, 256 devices: a whole 4x4x8 slice. The times are simulated.
256 devices in a mesh: rows: 32 (over x, z), cols: 8 (over y, core).
Axes of the slice: x: 4, y: 4, z: 8, core: 2. Of those that a mesh axis runs over, the one named last changes fastest.
Arguments:
- integrals: bfloat16 [32, 16, 64, 24576], P(None, None, 'rows', 'cols'), may hold values from -6 to 6
- density: bfloat16 [2048, 2048], P('cols', 'rows'), may hold values from -0.1875 to 0.1875
- neighbours: int32 [32, 16], replicated, may hold values from 0 to 31, all different within a row
- live: int32 [32], replicated, may hold values from 2 to 16, as said below
- sizes: int32 [32], replicated, may hold values from 48 to 64, as said below
Outputs:
- contracted: bfloat16 [32, 16, 64, 24576], P('rows', None, None, 'cols')
Inputs may be any that keep to these rules, and one draw needn't show every extreme that they name: `neighbours`: each row names 16 different blocks; every block is named by some row. Some block has all 16 slots live. `sizes`: some block has 64 functions.
All inputs are finite; a program needn't handle non-finite values.
Results may differ from a plain program's by a relative error of at most 0.001.
Values may be sent and summed in bfloat16 or wider, within the bound.
A program may use at most 128 MiB of HBM per device.

v0:
```python
import jax
import jax.numpy as jnp
from jax import lax
from jax.sharding import PartitionSpec as P

BS = 64


def shards(integrals, density, neighbours, live, sizes):
    row_count = lax.axis_size("rows")
    slot_count = neighbours.shape[1]
    local_blocks = integrals.shape[0] // row_count
    first_block = lax.axis_index("rows") * local_blocks
    partners_here = lax.dynamic_slice_in_dim(neighbours, first_block, local_blocks, 0)
    counts_here = lax.dynamic_slice_in_dim(live, first_block, local_blocks, 0)
    slot_index = jnp.arange(slot_count * BS, dtype=jnp.int32) // BS
    inner_index = jnp.arange(slot_count * BS, dtype=jnp.int32) % BS
    partner_blocks = partners_here[:, slot_index]
    positions = partner_blocks * BS + inner_index[None, :]
    usable = (
        (slot_index[None, :] < counts_here[:, None])
        & (inner_index[None, :] < sizes[partner_blocks])
    ).astype(jnp.bfloat16)
    nothing = jnp.zeros((), jnp.bfloat16)
    row_panel = lax.all_gather(density, "rows", axis=1, tiled=True)
    panel = lax.all_gather(row_panel, "cols", axis=0, tiled=True)
    inside = (positions >= 0) & (positions < panel.shape[0])
    clipped = jnp.clip(positions, 0, panel.shape[0] - 1)
    picked = jax.vmap(
        lambda row_list, col_list: jnp.take(jnp.take(panel, row_list, axis=0), col_list, axis=1)
    )(clipped, positions)
    selected = jnp.where(inside[:, :, None], picked, nothing)
    selected = selected * usable[:, :, None] * usable[:, None, :]
    width = integrals.shape[3]
    keep = ((jnp.arange(width, dtype=jnp.int32) % BS)[None, :] < sizes[:, None]).astype(
        jnp.bfloat16
    )
    outgoing = integrals * keep[:, None, None, :]
    received = lax.all_to_all(outgoing, "rows", split_axis=0, concat_axis=2, tiled=True)
    flat = received.reshape(received.shape[0], slot_count * BS, received.shape[3])
    product = jnp.einsum("btu,btw->buw", selected, flat, preferred_element_type=jnp.float32)
    return product.astype(jnp.bfloat16).reshape(
        received.shape[0], slot_count, BS, received.shape[3]
    )


def solution(mesh):
    return jax.shard_map(
        shards,
        mesh=mesh,
        in_specs=(P(None, None, "rows", "cols"), P("cols", "rows"), P(), P(), P()),
        out_specs=P("rows", None, None, "cols"),
        check_vma=False,
    )
```

profile of v0, /device:TPU:8, one launch (start us, length us, event | category | flops | bytes accessed | tf_op | source)
XLA Modules:
  0.0 321.1 jit_solution(15880701616481740260)
XLA Ops:
  6.5 0.7 all-gather.3.cloned.1.call-update
  7.3 0.0 all-gather.5.cloned.1.call-start
  7.3 81.6 %all-gather.3.cloned.1.call-done = bf16[256,2048]{0,1:T(8,128)(2,1)} async-done(((bf16[256,64]{0,1:T(8,128)(2,1)}), bf16[256,2048]{0,1:T(8,128)(2,1)}) %all-gather.3.cloned.1.call-update) | async-done | bytes 1048592 | tf_op jit(solution)/shard_map/all_gather | solution.py:25
  88.9 2.3 copy.11
  91.2 0.8 compare_convert_fusion
  92.0 7.5 %broadcast_multiply_fusion = bf16[32,16,2,3072]{3,2,1,0:T(2,128)(2,1)} fusion(bf16[32,16,2,3072]{3,2,1,0:T(2,128)(2,1)} %param.5, bf16[32,3072]{1,0:T(8,128)(2,1)S(1)} %compare_convert_fusion), kind=kLoop, calls=%fused_computation.4 | loop fusion | flops 3145728 | bytes 12779520 | tf_op jit(solution)/shard_map/mul | solution.py:38
  99.5 6.5 %all-to-all-start = ((bf16[32,16,2,3072]{3,2,1,0:T(2,128)(2,1)}), bf16[32,16,2,3072]{3,2,1,0:T(2,128)(2,1)}, u32[]{:S(2)}, u32[]{:S(2)}) async-start(bf16[32,16,2,3072]{3,2,1,0:T(2,128)(2,1)} %broadcast_multiply_fusion), calls=%async_computation | async-start | bytes 12582912 | tf_op jit(solution)/shard_map/all_to_all | solution.py:39
  106.0 0.6 dynamic_slice.7
  106.6 0.7 fusion.29
  107.6 4.4 %compare_select_fusion.10 = s32[1024,1]{0,1:T(1,128)S(1)} fusion(s32[]{:T(128)} %bitcast.9, s32[]{:T(128)} %bitcast.10, s32[]{:T(128)} %bitcast.11, s32[]{:T(128)} %bitcast.12, s32[]{:T(128)} %bitcast.13, s32[]{:T(128)} %bitcast.15, s32[]{:T(128)} %bitcast.14), kind=kLoop, calls=%fused_computation.62 | loop fusion | flops 23552 | bytes 4124 | tf_op jit(solution)/shard_map/gather | solution.py:18
  112.1 0.7 fusion.31
  112.8 5.5 %compare_and_fusion.2 = (pred[1024]{0:T(1024)(128)(4,1)S(1)}, s32[1024]{0:T(1024)S(1)}) fusion(pred[1024]{0:T(1024)(128)(4,1)S(1)} %compare_reduce_fusion.25, pred[1024]{0:T(1024)(128)(4,1)S(1)} %compare_reduce_fusion.26, pred[1024]{0:T(1024)(128)(4,1)S(1)} %compare_reduce_fusion.27, pred[1024]{0:T(1024)(128)(4,1)S(1)} %compare_reduce_fusion.28, ...), kind=kLoop, calls=%fused_computation.104 | loop fusion | flops 20480 | bytes 18468 | tf_op jit(solution)/shard_map/and | solution.py:27
  118.3 4.4 %compare_select_fusion.4 = (s32[1,1024,1]{1,2,0:T(1,128)S(1)}, s32[1,1024,1]{1,2,0:T(1,128)S(1)}, s32[1,1024,1]{1,2,0:T(1,128)S(1)}, s32[1,1024,1]{1,2,0:T(1,128)S(1)}) fusion(s32[]{:T(128)} %bitcast.50, s32[]{:T(128)} %bitcast.51, s32[]{:T(128)} %bitcast.52, s32[]{:T(128)} %bitcast.53, s32[]{:T(128)} %bitcast.54, s32[]{:T(128)} %bitcast.56, s32[]{:T(128)} %bitcast.55, ...), kind=kLoop, calls=%fused_computation.47 | loop fusion | flops 26624 | bytes 20508 | tf_op jit(solution)/shard_map/gather | solution.py:22
  122.8 0.7 fusion.30
  123.5 0.3 compare_reduce_fusion.24
  123.8 16.2 %fusion.25 = bf16[1024]{0:T(1024)(128)(2,1)S(1)} fusion(pred[1024]{0:T(1024)(128)(4,1)S(1)} %get-tuple-element.29, pred[1024]{0:T(1024)(128)(4,1)S(1)} %get-tuple-element.28, pred[1024]{0:T(1024)(128)(4,1)S(1)} %get-tuple-element.27, pred[1024]{0:T(1024)(128)(4,1)S(1)} %get-tuple-element.26, pred[1024]{0:T(1024)(128)(4,1)S(1)} %get-tuple-element.25, ...), kind=kLoop, calls=%fused_computation.101 | loop fusion | flops 41984 | bytes 31848 | tf_op jit(solution)/shard_map/convert_element_type | solution.py:23
  140.0 103.5 %all-to-all-done = bf16[32,16,2,3072]{3,2,1,0:T(2,128)(2,1)} async-done(((bf16[32,16,2,3072]{3,2,1,0:T(2,128)(2,1)}), bf16[32,16,2,3072]{3,2,1,0:T(2,128)(2,1)}, u32[]{:S(2)}, u32[]{:S(2)}) %all-to-all-start) | async-done | bytes 6291488 | tf_op jit(solution)/shard_map/all_to_all | solution.py:39
  243.5 6.8 %copy.13 = bf16[1,16,32,2,3072]{4,3,2,1,0:T(2,128)(2,1)} copy(bf16[1,16,32,2,3072]{4,3,1,2,0:T(2,128)(2,1)} %bitcast.60) | data formatting | bytes 12582912 | tf_op jit(solution)/shard_map/all_to_all | solution.py:39
  250.3 13.6 %reshape.444 = bf16[1024,3072]{1,0:T(8,128)(2,1)} reshape(bf16[1,16,32,2,3072]{4,3,2,1,0:T(2,128)(2,1)} %copy.13) | data formatting | bytes 12582912 | tf_op jit(solution)/shard_map/reshape.12
  263.9 13.3 %gather_fusion = bf16[1024,2048]{1,0:T(8,128)(2,1)} fusion(bf16[2048,2048]{1,0:T(8,128)(2,1)} %all-gather.5.cloned.1.call-done, s32[1024]{0:T(1024)S(1)} %broadcast_clamp_fusion), kind=kCustom, calls=%fused_computation | custom fusion | bytes 8392704 | tf_op jit(solution)/shard_map/vmap(jit(_take))/gather | solution.py:30
  277.2 4.6 %bitcast_select_fusion = bf16[1,1024,2048]{2,1,0:T(8,128)(2,1)} fusion(bf16[1024,2048]{1,0:T(8,128)(2,1)} %gather_fusion, pred[1024]{0:T(1024)(128)(4,1)S(1)} %get-tuple-element.55), kind=kLoop, calls=%fused_computation.3 | loop fusion | flops 2097152 | bytes 8389632 | tf_op jit(solution)/shard_map/vmap(jit(_take))/select_n | solution.py:30
  281.8 6.4 %copy.12 = bf16[1,1024,2048]{1,2,0:T(8,128)(2,1)} copy(bf16[1,1024,2048]{2,1,0:T(8,128)(2,1)} %bitcast_select_fusion) | data formatting | bytes 8388608 | tf_op jit(solution)/shard_map/vmap(jit(_take))/select_n | solution.py:30
  288.2 14.2 %gather_fusion.1 = bf16[1024,1024]{1,0:T(8,128)(2,1)S(1)} fusion(bf16[1,1024,2048]{1,2,0:T(8,128)(2,1)} %copy.12, s32[1024]{0:T(1024)S(1)} %bitcast.79), kind=kCustom, calls=%fused_computation.1 | custom fusion | bytes 4202496 | tf_op jit(solution)/shard_map/vmap(jit(_take))/gather | solution.py:30
  302.5 11.8 %convolution_convert_fusion = bf16[1024,3072]{1,0:T(8,128)(2,1)} fusion(bf16[1024,3072]{1,0:T(8,128)(2,1)} %reshape.444, bf16[1024,1024]{1,0:T(8,128)(2,1)S(1)} %gather_fusion.1, pred[1024]{0:T(1024)(128)(4,1)S(1)} %get-tuple-element.54, pred[1024]{0:T(1024)(128)(4,1)S(1)} %get-tuple-element.32, bf16[1024]{0:T(1024)(128)(2,1)S(1)} %fusion.25), kind=kOutput, calls=%fused_computation.2 | convolution fusion | flops 6449790976 | bytes 14684160 | tf_op jit(solution)/shard_map/btu,btw->buw/dot_general | solution.py:41
  (24 shorter events, 0.4 us)
Async XLA Ops:
  6.5 82.4 %all-gather.3.cloned.1.call-start = ((), (), s32[]{:S(2)}) async-start(), calls=%async_computation.1 | async-start | bytes 1081344 | tf_op jit(solution)/shard_map/all_gather | solution.py:25
  7.3 256.7 %all-gather.5.cloned.1.call-start = ((), (), s32[]{:S(2)}) async-start(), calls=%async_computation.2 | async-start | bytes 9437184 | tf_op jit(solution)/shard_map/all_gather | solution.py:26
  99.5 6.5 %copy-start.2 = (s32[32]{0:T(128)S(1)}, s32[32]{0:T(128)}, u32[]{:S(2)}) copy-start(s32[32]{0:T(128)} %param.8) | copy-start | bytes 388
  99.5 7.1 %copy-start.1 = (s32[32,16]{0,1:T(8,128)S(1)}, s32[32,16]{0,1:T(8,128)}, u32[]{:S(2)}) copy-start(s32[32,16]{0,1:T(8,128)} %param.7) | copy-start | bytes 6148
  99.5 12.6 %copy-start = (s32[32]{0:T(128)S(1)}, s32[32]{0:T(128)}, u32[]{:S(2)}) copy-start(s32[32]{0:T(128)} %param.9) | copy-start | bytes 388
  99.5 144.0 %all-to-all-start = ((bf16[32,16,2,3072]{3,2,1,0:T(2,128)(2,1)}), bf16[32,16,2,3072]{3,2,1,0:T(2,128)(2,1)}, u32[]{:S(2)}, u32[]{:S(2)}) async-start(bf16[32,16,2,3072]{3,2,1,0:T(2,128)(2,1)} %broadcast_multiply_fusion), calls=%async_computation | async-start | bytes 12582912 | tf_op jit(solution)/shard_map/all_to_all | solution.py:39
Sparse Core Ops, SparseCore 0:
  10.0 78.9 all-gather.2
  91.4 49.1 all-gather.4
where the time goes:
time: 323 us; the launch traced here: 321 us
  waiting for transfers between devices  186 us (58%)
  local copies, waits for them, and re-layouts  59.4 us (18%)
  other arithmetic  44 us (14%)
  between operations  13.5 us (4%)
  matrix products  11.8 us (4%)
  starting transfers between devices  6.53 us (2%)
    all_to_all x1, waiting for transfers between devices, shards(): lax.all_to_all(outgoing, 'rows', split_axis=0, concat_axis=2, tiled=True)  103 us
    all_gather x1, waiting for transfers between devices, shards(): row_panel = lax.all_gather(density, 'rows', axis=1, tiled=True)  81.6 us
    convert_element_type x1, other arithmetic, shards(): usable = ((slot_index[None, :] < counts_here[:, None]) & (inner_index[Non...  16.2 us
    gather x2, local copies, waits for them, and re-layouts, shards(): jnp.take(jnp.take(panel, row_list, axis=0), col_list, axis=1)  14.2 us
    another operation x1, local copies, waits for them, and re-layouts  13.6 us
    gather x1, local copies, waits for them, and re-layouts, shards(): jnp.take(panel, row_list, axis=0)  13.3 us
    dot_general x1, matrix products, shards(): jnp.einsum('btu,btw->buw', selected, flat, preferred_element_type=jnp.flo...  11.8 us
    mul x1, other arithmetic, shards(): outgoing = integrals * keep[:, None, None, :]  7.46 us
  transfers between devices with their start and end apart: 3, of which 2 were waited for; matrix products, arithmetic and copies ran while one was open for 19% of the time, Pallas kernels for 0%

commit v1 on v0

v1 whole, which is shorter than its diff:
```python
import functools

import jax
import jax.numpy as jnp
from jax import lax
from jax.experimental import pallas as pl
from jax.experimental.pallas import tpu as pltpu
from jax.sharding import PartitionSpec as P

BS = 64
NX, NZ, NC = 4, 8, 8
NR = NX * NZ
MESH = pl.DeviceIdType.MESH


def exchange(x_ref, d_ref, neigh, live, sizes, r_ref, sel_ref, d1, mine, d2, xs, xr, zs, zr, qs, qr, ys, yr, local):
    row = lax.axis_index("rows")
    col = lax.axis_index("cols")
    x, z = row // NZ, row % NZ
    slots = neigh.shape[1]

    def at(dx, dz):
        return lax.rem(x + dx, NX) * NZ + lax.rem(z + dz, NZ)

    offsets = [(dx, dz) for dz in range(NZ) for dx in range(NX) if (dx, dz) != (0, 0)]
    barrier = pltpu.get_barrier_semaphore()
    for dx, dz in offsets:
        pl.semaphore_signal(barrier, inc=1, device_id=(at(dx, dz), col), device_id_type=MESH)
    for dc in range(1, NC):
        pl.semaphore_signal(barrier, inc=1, device_id=(row, lax.rem(col + dc, NC)), device_id_type=MESH)
    own = pltpu.make_async_copy(d_ref, d1.at[row], local.at[0])
    own.start()
    own_x = pltpu.make_async_copy(x_ref.at[row], r_ref.at[:, :, row], local.at[1])
    own_x.start()
    pl.semaphore_wait(barrier, len(offsets) + NC - 1)

    zcopies = []
    for i, dz in enumerate(range(1, NZ)):
        cp = pltpu.make_async_remote_copy(
            src_ref=d_ref, dst_ref=d1.at[row], send_sem=zs.at[i], recv_sem=zr.at[i],
            device_id=(at(0, dz), col), device_id_type=MESH)
        cp.start()
        zcopies.append(cp)
    copies = []
    for i, (dx, dz) in enumerate(offsets):
        to = at(dx, dz)
        cp = pltpu.make_async_remote_copy(
            src_ref=x_ref.at[to], dst_ref=r_ref.at[:, :, row], send_sem=xs.at[i], recv_sem=xr.at[i],
            device_id=(to, col), device_id_type=MESH)
        cp.start()
        copies.append(cp)

    own.wait()
    for cp in zcopies:
        cp.wait()
    xcopies = []
    for i, dx in enumerate(range(1, NX)):
        cp = pltpu.make_async_remote_copy(
            src_ref=d1.at[pl.ds(x * NZ, NZ)], dst_ref=d1.at[pl.ds(x * NZ, NZ)], send_sem=qs.at[i], recv_sem=qr.at[i],
            device_id=(at(dx, 0), col), device_id_type=MESH)
        cp.start()
        xcopies.append(cp)
    for cp in xcopies:
        cp.wait()

    inner = lax.broadcasted_iota(jnp.int32, (BS, 256), 0)
    for k in range(slots):
        other = neigh[row, k]
        limit = jnp.where(k < live[row], sizes[other], 0)
        mine[pl.ds(k * BS, BS), :] = jnp.where(inner < limit, d1[other], jnp.zeros((), jnp.bfloat16))

    ycopies = []
    for i, dc in enumerate(range(1, NC)):
        cp = pltpu.make_async_remote_copy(
            src_ref=mine, dst_ref=d2.at[col], send_sem=ys.at[i], recv_sem=yr.at[i],
            device_id=(row, lax.rem(col + dc, NC)), device_id_type=MESH)
        cp.start()
        ycopies.append(cp)
    d2[col] = mine[...]
    for cp in ycopies:
        cp.wait()

    wide = slots * BS
    lane = lax.broadcasted_iota(jnp.int32, (1, wide), 1)
    position = jnp.full((1, wide), -1, jnp.int32)
    for k in range(slots):
        other = neigh[row, k]
        limit = jnp.where(k < live[row], sizes[other], 0)
        here = (lane >= k * BS) & (lane < k * BS + limit)
        position = jnp.where(here, other * BS + lane - k * BS, position)

    @pl.loop(0, wide // 256)
    def _(part):
        rows_here = pl.ds(pl.multiple_of(part * 256, 256), 256)
        total = jnp.zeros((256, wide), jnp.float32)
        for c in range(NC):
            index = lax.broadcasted_iota(jnp.int32, (256, wide), 0) + c * 256
            pick = jnp.where(index == position, 1.0, 0.0).astype(jnp.bfloat16)
            total = total + jnp.dot(d2[c, rows_here, :], pick, preferred_element_type=jnp.float32)
        sel_ref[rows_here, :] = total.astype(jnp.bfloat16)

    own_x.wait()
    for cp in copies:
        cp.wait()


def contract(tiles, sizes, sel_ref, r_ref, o_ref):
    size = sizes[lax.axis_index("rows")]
    lane = lax.broadcasted_iota(jnp.int32, (1, 128), 1)
    keep = lax.rem(lane, BS) < size
    for pair in range(tiles // 2):
        rhs = jnp.concatenate(
            [r_ref[:, 2 * pair + h].reshape(r_ref.shape[0] * BS, 128) for h in range(2)], axis=1)
        out = jnp.dot(sel_ref[...], rhs, preferred_element_type=jnp.float32)
        for h in range(2):
            part = jnp.where(keep, out[:, h * 128:(h + 1) * 128], 0.0).astype(jnp.bfloat16)
            lanes = pl.ds((2 * pair + h) * 128, 128)
            o_ref[0, :, :, lanes] = part.reshape(r_ref.shape[0], BS, 128)


def shards(integrals, density, neighbours, live, sizes):
    blocks, slots, rows_each, width = integrals.shape
    lanes = width // 128
    view = integrals.reshape(blocks, slots, rows_each, lanes, 128).transpose(0, 1, 3, 2, 4)
    dma = pltpu.SemaphoreType.DMA
    smem = pl.BlockSpec(memory_space=pltpu.SMEM)
    anywhere = pl.BlockSpec(memory_space=pl.ANY)
    vmem = pl.BlockSpec(memory_space=pltpu.VMEM)
    wide = slots * BS
    received, selected = pl.pallas_call(
        exchange,
        out_shape=(
            jax.ShapeDtypeStruct((slots, lanes, blocks, rows_each, 128), jnp.bfloat16),
            jax.ShapeDtypeStruct((wide, wide), jnp.bfloat16),
        ),
        in_specs=[anywhere, vmem, smem, smem, smem],
        out_specs=(anywhere, vmem),
        scratch_shapes=[
            pltpu.VMEM((NR, BS, 256), jnp.bfloat16),
            pltpu.VMEM((wide, 256), jnp.bfloat16),
            pltpu.VMEM((NC, wide, 256), jnp.bfloat16),
            dma((NR - 1,)), dma((NR - 1,)),
            dma((NZ - 1,)), dma((NZ - 1,)),
            dma((NX - 1,)), dma((NX - 1,)),
            dma((NC - 1,)), dma((NC - 1,)),
            dma((2,)),
        ],
        compiler_params=pltpu.CompilerParams(
            collective_id=0, has_side_effects=True, vmem_limit_bytes=40 * 2**20),
        name="exchange",
    )(view, density.T, neighbours, live, sizes)
    flat = received.reshape(slots, lanes, blocks * rows_each, 128)
    tiles = 4
    return pl.pallas_call(
        functools.partial(contract, tiles),
        grid=(lanes // tiles,),
        in_specs=[
            smem,
            pl.BlockSpec((wide, wide), lambda i: (0, 0)),
            pl.BlockSpec((slots, tiles, BS, 128), lambda i: (0, i, 0, 0)),
        ],
        out_specs=pl.BlockSpec((1, slots, BS, tiles * 128), lambda i: (0, 0, 0, i)),
        out_shape=jax.ShapeDtypeStruct((1, slots, BS, width), jnp.bfloat16),
        compiler_params=pltpu.CompilerParams(vmem_limit_bytes=40 * 2**20),
        name="contract",
    )(sizes, selected, flat)


def solution(mesh):
    return jax.shard_map(
        shards,
        mesh=mesh,
        in_specs=(P(None, None, "rows", "cols"), P("cols", "rows"), P(), P(), P()),
        out_specs=P("rows", None, None, "cols"),
        check_vma=False,
    )
```

time: 323 us -> 176 us (0.54)
  the two profiles are of different devices: /device:TPU:8 before, /device:TPU:208 now
where the time goes in v1:
time: 176 us; the launch traced here: 175 us
  Pallas kernels  173 us (98%)
  local copies, waits for them, and re-layouts  2.84 us (2%)
    pallas_call x1, Pallas kernels, shards(): pl.pallas_call(exchange, out_shape=(jax.ShapeDtypeStruct((slots, lanes, b...  163 us
    pallas_call x1, Pallas kernels, shards(): pl.pallas_call(functools.partial(contract, tiles), grid=(lanes // tiles,)...  9.53 us

profile of v1, /device:TPU:208, one launch (start us, length us, event | category | flops | bytes accessed | tf_op | source)
XLA Modules:
  0.0 175.5 jit_solution(17142447859095985849)
XLA Ops:
  0.0 0.8 copy.6.neigh
  0.8 0.0 copy-start
  0.8 0.8 copy-done
  1.5 0.0 copy-start.1
  1.5 0.7 copy-done.1
  2.2 0.0 copy-start.2
  2.2 0.7 copy-done.2
  2.8 163.1 %exchange.1 = (bf16[16,24,32,2,128]{4,3,2,1,0:T(2,128)(2,1)S(1)}, bf16[1024,1024]{1,0:T(8,128)(2,1)S(1)}) custom-call(bf16[32,16,24,2,128]{4,3,2,1,0:T(2,128)(2,1)} %bitcast.7, bf16[64,256]{1,0:T(8,128)(2,1)S(1)} %bitcast.6, s32[32,16]{1,0:T(8,128)S(1)} %copy.6.neigh, s32[32]{0:T(128)S(1)} %copy-done.2, s32[32]{0:T(128)S(1)} %copy-done.1), custom_call_target="tpu_custom_call" | custom-call | tf_op jit(solution)/shard_map/exchange/pallas_call | solution.py:130
  165.9 9.5 %contract.1 = bf16[1,16,64,3072]{3,2,1,0:T(8,128)(2,1)} custom-call(s32[32]{0:T(128)S(1)} %copy-done.1, bf16[1024,1024]{1,0:T(8,128)(2,1)S(1)} %get-tuple-element.7.sel_ref, bf16[16,24,64,128]{3,2,1,0:T(8,128)(2,1)S(1)} %bitcast.5), custom_call_target="tpu_custom_call" | custom-call | tf_op jit(solution)/shard_map/contract/pallas_call | solution.py:154
Async XLA Ops:
  0.8 0.8 copy-start
  1.5 0.7 copy-start.1
  2.2 0.7 copy-start.2

commit v2 on v1

v2 whole, which is shorter than its diff:
```python
import functools

import jax
import jax.numpy as jnp
from jax import lax
from jax.experimental import pallas as pl
from jax.experimental.pallas import tpu as pltpu
from jax.sharding import PartitionSpec as P

BS = 64
NX, NZ, NC = 4, 8, 8
NR = NX * NZ
MESH = pl.DeviceIdType.MESH
CHUNKS = (3, 5, 5, 4, 3, 2, 1, 1)
FIRST = tuple(sum(CHUNKS[:i]) for i in range(len(CHUNKS)))
AHEAD = 2
ZSTEPS = (4, 3, 5, 2, 6, 1, 7)
XSTEPS = (2, 1, 3)
CAPACITIES = tuple(range(36, 65, 4))


def exchange(capacity, x_ref, d_ref, table, neigh, live, sizes, r_ref, sel_ref, d1, mine, d2, *rest):
    n = len(CHUNKS)
    x_in, z_send, z_recv, x_send = (rest[i * n:(i + 1) * n] for i in range(4))
    in_sem, zss, zrs, xss, xrs, own_sem, zs, zr, qs, qr, ys, yr, dsem = rest[4 * n:]
    row = lax.axis_index("rows")
    col = lax.axis_index("cols")
    x, z = row // NZ, lax.rem(row, NZ)
    slots = neigh.shape[1]
    units = NX * slots

    def at(dx, dz):
        return lax.rem(x + dx, NX) * NZ + lax.rem(z + dz, NZ)

    loads = []
    for c in range(n):
        cp = pltpu.make_async_copy(x_ref.at[:, pl.ds(FIRST[c], CHUNKS[c])], x_in[c], in_sem.at[c])
        cp.start()
        loads.append(cp)
    own_d = pltpu.make_async_copy(d_ref, d1.at[row], dsem)
    own_d.start()

    barrier = pltpu.get_barrier_semaphore()
    for dz in ZSTEPS:
        pl.semaphore_signal(barrier, inc=1, device_id=(at(0, dz), col), device_id_type=MESH)
    for dx in XSTEPS:
        pl.semaphore_signal(barrier, inc=1, device_id=(at(dx, 0), col), device_id_type=MESH)
    for dc in range(1, NC):
        pl.semaphore_signal(barrier, inc=1, device_id=(row, lax.rem(col + dc, NC)), device_id_type=MESH)
    pl.semaphore_wait(barrier, NZ + NX + NC - 3)

    def pack(c):
        loads[c].wait()

        @pl.loop(0, capacity)
        def _(s):
            z_recv[c][z, s] = x_in[c][table[z, s]]
            for i, dz in enumerate(ZSTEPS):
                z_send[c][i, s] = x_in[c][table[lax.rem(z + dz, NZ), s]]

    def send_z(c):
        out = []
        for i, dz in enumerate(ZSTEPS):
            cp = pltpu.make_async_remote_copy(
                src_ref=z_send[c].at[i], dst_ref=z_recv[c].at[z], send_sem=zss.at[c, i], recv_sem=zrs.at[c, i],
                device_id=(at(0, dz), col), device_id_type=MESH)
            cp.start()
            out.append(cp)
        return out

    def unpack(c):
        @pl.loop(0, units)
        def _(p):
            place = table[NZ + z, p]
            for other in range(NZ):
                x_send[c][p, :, other] = z_recv[c][other, place]

    def send_x(c):
        out = []
        lanes = pl.ds(FIRST[c], CHUNKS[c])
        for i, dx in enumerate(XSTEPS):
            xp = lax.rem(x + dx, NX)
            cp = pltpu.make_async_remote_copy(
                src_ref=x_send[c].at[pl.ds(xp * slots, slots)], dst_ref=r_ref.at[:, lanes, pl.ds(x * NZ, NZ)],
                send_sem=xss.at[c, i], recv_sem=xrs.at[c, i],
                device_id=(at(dx, 0), col), device_id_type=MESH)
            cp.start()
            out.append(cp)
        cp = pltpu.make_async_copy(
            x_send[c].at[pl.ds(x * slots, slots)], r_ref.at[:, lanes, pl.ds(x * NZ, NZ)], own_sem.at[c])
        cp.start()
        out.append(cp)
        return out

    d_copies = []
    for i, dz in enumerate(ZSTEPS):
        cp = pltpu.make_async_remote_copy(
            src_ref=d_ref, dst_ref=d1.at[row], send_sem=zs.at[i], recv_sem=zr.at[i],
            device_id=(at(0, dz), col), device_id_type=MESH)
        cp.start()
        d_copies.append(cp)

    z_copies, x_copies = [], []
    for c in range(AHEAD):
        pack(c)
        z_copies.append(send_z(c))
    own_d.wait()
    for cp in d_copies:
        cp.wait()
    d_copies = []
    for i, dx in enumerate(XSTEPS):
        cp = pltpu.make_async_remote_copy(
            src_ref=d1.at[pl.ds(x * NZ, NZ)], dst_ref=d1.at[pl.ds(x * NZ, NZ)], send_sem=qs.at[i], recv_sem=qr.at[i],
            device_id=(at(dx, 0), col), device_id_type=MESH)
        cp.start()
        d_copies.append(cp)
    for c in range(AHEAD, n):
        pack(c)

    def density_rows():
        for cp in d_copies:
            cp.wait()
        inner = lax.broadcasted_iota(jnp.int32, (BS, 256), 0)
        for k in range(slots):
            other = neigh[row, k]
            limit = jnp.where(k < live[row], sizes[other], 0)
            mine[pl.ds(k * BS, BS), :] = jnp.where(inner < limit, d1[other], jnp.zeros((), jnp.bfloat16))
        out = []
        for i, dc in enumerate(range(1, NC)):
            cp = pltpu.make_async_remote_copy(
                src_ref=mine, dst_ref=d2.at[col], send_sem=ys.at[i], recv_sem=yr.at[i],
                device_id=(row, lax.rem(col + dc, NC)), device_id_type=MESH)
            cp.start()
            out.append(cp)
        d2[col] = mine[...]
        return out

    def density_columns():
        wide = slots * BS
        lane = lax.broadcasted_iota(jnp.int32, (1, wide), 1)
        position = jnp.full((1, wide), -1, jnp.int32)
        for k in range(slots):
            other = neigh[row, k]
            limit = jnp.where(k < live[row], sizes[other], 0)
            here = (lane >= k * BS) & (lane < k * BS + limit)
            position = jnp.where(here, other * BS + lane - k * BS, position)

        @pl.loop(0, wide // 256)
        def _(part):
            rows_here = pl.ds(pl.multiple_of(part * 256, 256), 256)
            total = jnp.zeros((256, wide), jnp.float32)
            for c in range(NC):
                index = lax.broadcasted_iota(jnp.int32, (256, wide), 0) + c * 256
                pick = jnp.where(index == position, 1.0, 0.0).astype(jnp.bfloat16)
                total = total + jnp.dot(d2[c, rows_here, :], pick, preferred_element_type=jnp.float32)
            sel_ref[rows_here, :] = total.astype(jnp.bfloat16)

    for c in range(n):
        for cp in z_copies[c]:
            cp.wait()
        if c + AHEAD < n:
            z_copies.append(send_z(c + AHEAD))
        unpack(c)
        x_copies += send_x(c)
        if c == 0:
            d_copies = density_rows()
        if c == 4:
            for cp in d_copies:
                cp.wait()
            density_columns()
    for cp in x_copies:
        cp.wait()


def contract(tiles, sizes, sel_ref, r_ref, o_ref):
    size = sizes[lax.axis_index("rows")]
    lane = lax.broadcasted_iota(jnp.int32, (1, 128), 1)
    keep = lax.rem(lane, BS) < size
    for pair in range(tiles // 2):
        rhs = jnp.concatenate(
            [r_ref[:, 2 * pair + h].reshape(r_ref.shape[0] * BS, 128) for h in range(2)], axis=1)
        out = jnp.dot(sel_ref[...], rhs, preferred_element_type=jnp.float32)
        for h in range(2):
            part = jnp.where(keep, out[:, h * 128:(h + 1) * 128], 0.0).astype(jnp.bfloat16)
            lanes = pl.ds((2 * pair + h) * 128, 128)
            o_ref[0, :, :, lanes] = part.reshape(r_ref.shape[0], BS, 128)


def tables(live, slots):
    counts = live.reshape(NX, NZ)
    ends = [counts[0]]
    for i in range(1, NX):
        ends.append(ends[-1] + counts[i])
    starts = [jnp.zeros_like(ends[0])] + ends[:-1]
    place = jnp.arange(NX * slots, dtype=jnp.int32)[None, :]
    target = jnp.arange(NZ, dtype=jnp.int32)[:, None]
    unit = jnp.zeros((NZ, NX * slots), jnp.int32)
    back = jnp.zeros((NZ, NX * slots), jnp.int32)
    for i in range(NX):
        start, end = starts[i][:, None], ends[i][:, None]
        unit = jnp.where((place >= start) & (place < end), (i * NZ + target) * slots + place - start, unit)
        slot = jnp.minimum(place - i * slots, end - start - 1)
        back = jnp.where((place >= i * slots) & (place < (i + 1) * slots), start + jnp.maximum(slot, 0), back)
    return jnp.concatenate([unit, back], axis=0), jnp.max(ends[-1])


def shards(integrals, density, neighbours, live, sizes):
    blocks, slots, rows_each, width = integrals.shape
    lanes = width // 128
    view = integrals.reshape(blocks * slots, rows_each, lanes, 128).transpose(0, 2, 1, 3)
    dma = pltpu.SemaphoreType.DMA
    smem = pl.BlockSpec(memory_space=pltpu.SMEM)
    anywhere = pl.BlockSpec(memory_space=pl.ANY)
    vmem = pl.BlockSpec(memory_space=pltpu.VMEM)
    wide = slots * BS
    n = len(CHUNKS)
    table, most = tables(live, slots)

    def call(which, capacity, *operands):
        def buffers(*lead):
            return [pltpu.VMEM(lead + (q, rows_each, 128), jnp.bfloat16) for q in CHUNKS]

        return pl.pallas_call(
            functools.partial(exchange, capacity),
            out_shape=(
                jax.ShapeDtypeStruct((slots, lanes, blocks, rows_each, 128), jnp.bfloat16),
                jax.ShapeDtypeStruct((wide, wide), jnp.bfloat16),
            ),
            in_specs=[anywhere, vmem, smem, smem, smem, smem],
            out_specs=(anywhere, vmem),
            scratch_shapes=[
                pltpu.VMEM((NR, BS, 256), jnp.bfloat16),
                pltpu.VMEM((wide, 256), jnp.bfloat16),
                pltpu.VMEM((NC, wide, 256), jnp.bfloat16),
                *buffers(blocks * slots), *buffers(NZ - 1, capacity), *buffers(NZ, capacity),
                *[pltpu.VMEM((NX * slots, q, NZ, rows_each, 128), jnp.bfloat16) for q in CHUNKS],
                dma((n,)),
                dma((n, NZ - 1)), dma((n, NZ - 1)),
                dma((n, NX - 1)), dma((n, NX - 1)),
                dma((n,)),
                dma((NZ - 1,)), dma((NZ - 1,)),
                dma((NX - 1,)), dma((NX - 1,)),
                dma((NC - 1,)), dma((NC - 1,)),
                dma,
            ],
            compiler_params=pltpu.CompilerParams(
                collective_id=which, has_side_effects=True, vmem_limit_bytes=56 * 2**20),
            name="exchange",
        )(*operands)

    which = jnp.clip((most - CAPACITIES[0] + 3) // 4, 0, len(CAPACITIES) - 1)
    received, selected = lax.switch(
        which, [functools.partial(call, i, capacity) for i, capacity in enumerate(CAPACITIES)],
        view, density.T, table, neighbours, live, sizes)
    flat = received.reshape(slots, lanes, blocks * rows_each, 128)
    tiles = 4
    return pl.pallas_call(
        functools.partial(contract, tiles),
        grid=(lanes // tiles,),
        in_specs=[
            smem,
            pl.BlockSpec((wide, wide), lambda i: (0, 0)),
            pl.BlockSpec((slots, tiles, BS, 128), lambda i: (0, i, 0, 0)),
        ],
        out_specs=pl.BlockSpec((1, slots, BS, tiles * 128), lambda i: (0, 0, 0, i)),
        out_shape=jax.ShapeDtypeStruct((1, slots, BS, width), jnp.bfloat16),
        compiler_params=pltpu.CompilerParams(vmem_limit_bytes=40 * 2**20),
        name="contract",
    )(sizes, selected, flat)


def solution(mesh):
    return jax.shard_map(
        shards,
        mesh=mesh,
        in_specs=(P(None, None, "rows", "cols"), P("cols", "rows"), P(), P(), P()),
        out_specs=P("rows", None, None, "cols"),
        check_vma=False,
    )
```

time: 176 us -> 145 us (0.82)
  the two profiles are of different devices: /device:TPU:208 before, /device:TPU:8 now
where the time goes in v2:
time: 145 us; the launch traced here: 143 us
  Pallas kernels  138 us (95%)
  other arithmetic  1.64 us (1%)
    pallas_call x1, Pallas kernels, call(): pl.pallas_call(functools.partial(exchange, capacity), out_shape=(jax.Shap...  128 us
    pallas_call x1, Pallas kernels, shards(): pl.pallas_call(functools.partial(contract, tiles), grid=(lanes // tiles,)...  10.6 us

profile of v2, /device:TPU:8, one launch (start us, length us, event | category | flops | bytes accessed | tf_op | source)
XLA Modules:
  0.0 142.9 jit_solution(9118144971996862932)
XLA Ops:
  0.1 1.5 %fusion.4 = (s32[8]{0:T(128)S(1)}, s32[8]{0:T(128)S(1)}, s32[8]{0:T(128)S(1)}, s32[8]{0:T(128)S(1)}, s32[8]{0:T(128)S(1)}, /*index=5*/s32[]{:T(128)}, s32[8]{0:T(128)S(1)}, s32[8]{0:T(128)S(1)}, s32[8]{0:T(128)S(1)}) fusion(s32[32]{0:T(128)} %param.16), kind=kLoop, calls=%fused_computation.32 | loop fusion | flops 63 | bytes 388 | tf_op jit(solution)/shard_map/slice | solution.py:191
  2.2 0.1 select_select_fusion.1
  2.4 129.9 %conditional.1 = (bf16[1024,1024]{1,0:T(8,128)(2,1)}, bf16[16,24,64,128]{3,2,1,0:T(8,128)(2,1)S(1)}) conditional(s32[]{:T(128)} %clamp.3, (bf16[512,24,2,128]{3,2,1,0:T(2,128)(2,1)}, bf16[64,256]{1,0:T(8,128)(2,1)}, s32[16,64]{1,0:T(8,128)S(1)}, s32[32,16]{0,1:T(8,128)}, s32[32]{0:T(128)}, ...), branch_computations={%region_1.2_spmd, %region_2.3_spmd, %region_3.4_spmd, %region_4.5_... | conditional | bytes 4112 | solution.py:252
  2.6 1.4 copy.9.neigh
  4.0 127.8 %exchange.11 = (bf16[16,24,32,2,128]{4,3,2,1,0:T(2,128)(2,1)S(1)}, bf16[1024,1024]{1,0:T(8,128)(2,1)}) custom-call(bf16[512,24,2,128]{3,2,1,0:T(2,128)(2,1)} %get-tuple-element.142.x_ref, bf16[64,256]{1,0:T(8,128)(2,1)} %get-tuple-element.143.d_ref, s32[16,64]{1,0:T(8,128)S(1)} %get-tuple-element.144.table, s32[32,16]{1,0:T(8,128)} %copy.9.neigh, ...), custom_call_target="tpu_custom_call" | custom-call | tf_op jit(solution)/shard_map/cond/branch_3_fun/exchange/pallas_call | solution.py:223
  132.3 10.6 %contract.1 = bf16[1,16,64,3072]{3,2,1,0:T(8,128)(2,1)} custom-call(s32[32]{0:T(128)} %sizes.1, bf16[1024,1024]{1,0:T(8,128)(2,1)} %get-tuple-element.184.sel_ref, bf16[16,24,64,128]{3,2,1,0:T(8,128)(2,1)S(1)} %get-tuple-element.185.r_ref), custom_call_target="tpu_custom_call" | custom-call | tf_op jit(solution)/shard_map/contract/pallas_call | solution.py:257
  (7 shorter events, 0.0 us)
